TPU v7x, 32 devices: a whole 2x2x4 slice. The times are simulated.
32 devices in a mesh: group: 2 (over x), vocab: 8 (over z, y), dp: 2 (over core).
Axes of the slice: x: 2, y: 2, z: 4, core: 2. Of those that a mesh axis runs over, the one named last changes fastest.
Arguments:
- hidden_rows: bfloat16 [256, 4096], P(('vocab', 'dp')), may hold values from -96 to 96
- lm_head: bfloat16 [4096, 20480], P(None, ('vocab', 'dp')), may hold values from -1 to 1
- draft_len: int32 [128], P(('group', 'vocab', 'dp')), parts along dimension 0, may hold values from 1 to 3, as said below
- draft_tokens: int32 [64, 3], P(('vocab', 'dp')), may hold values from 0 to 20479
- draft_prob: float32 [64, 3], P(('vocab', 'dp')), may hold values from 0.05 to 1
- accept_uniform: float32 [128, 3], P(('group', 'vocab', 'dp')), parts along dimension 0, may hold values from 0 to 1
Outputs:
- accept_ratio: float32 [128, 3], P(('group', 'vocab', 'dp')), parts along dimension 0
- accepted: int32 [128], P(('group', 'vocab', 'dp')), parts along dimension 0
- correction: float32 [128, 20480], P(('group', 'vocab', 'dp')), parts along dimension 0
There are 2 independent parts, one for each index of `group`. A program takes and returns all parts, laid end to end along the dimension named above; an argument that names none is the same for every part. Nothing has to cross between parts.
Inputs may be any that keep to these rules, and one draw needn't show every extreme that they name: In each aligned block of 4 requests (the requests of one device), draft_len sums to at most 8, and exactly that in at least one block of every draw.
All inputs are finite; a program needn't handle non-finite values.
Results may differ from a plain program's by a relative error of at most 0.0003.
Values may be sent and summed in bfloat16 or wider, within the bound.
A program may use at most 128 MiB of HBM per device.

v0:
```python
import jax
import jax.numpy as jnp
from jax import lax
from jax.sharding import PartitionSpec as P


def body(hidden_rows, lm_head, draft_len, draft_tokens, draft_prob, accept_uniform):
    device_count = lax.axis_size(("vocab", "dp"))
    my_index = lax.axis_index(("vocab", "dp"))
    req_dev = draft_len.shape[0]
    slots = hidden_rows.shape[0] // req_dev
    drafts = slots - 1
    columns = lm_head.shape[1]
    vocab_all = columns * device_count
    all_len, all_tokens = (
        lax.all_gather(draft_len, ("vocab", "dp"), axis=0, tiled=True),
        lax.all_gather(draft_tokens, ("vocab", "dp"), axis=0, tiled=True),
    )
    all_prob, all_uniform = (
        lax.all_gather(draft_prob, ("vocab", "dp"), axis=0, tiled=True),
        lax.all_gather(accept_uniform, ("vocab", "dp"), axis=0, tiled=True),
    )
    request_total = req_dev * device_count
    request_ids = jnp.arange(request_total, dtype=jnp.int32)
    slot_ids = jnp.arange(slots, dtype=jnp.int32)
    logits = jnp.dot(
        lax.all_gather(hidden_rows, ("vocab", "dp"), axis=0, tiled=True),
        lm_head,
        preferred_element_type=jnp.float32,
    )
    row_of = request_ids[:, None] * slots + slot_ids[None, :]
    local_max = jnp.max(logits, axis=1)
    draft_rows = row_of[:, :drafts]
    shifted = all_tokens - my_index * columns
    inside = (shifted >= 0) & (shifted < columns)
    picked = jnp.where(inside, logits[draft_rows, jnp.clip(shifted, 0, columns - 1)], 0.0)
    row_max = lax.pmax(local_max, ("vocab", "dp"))
    local_total = jnp.sum(jnp.exp(logits - row_max[:, None]), axis=1)
    row_total, drafted = lax.psum((local_total, picked), ("vocab", "dp"))
    p_draft = jnp.exp(drafted - row_max[draft_rows]) / row_total[draft_rows]
    live_slot = jnp.arange(drafts, dtype=jnp.int32)[None, :] < all_len[:, None]
    accept_ratio = jnp.where(live_slot, jnp.minimum(1.0, p_draft / all_prob), 0.0)
    passed = (all_uniform < accept_ratio).astype(jnp.int32)
    accepted = jnp.sum(jnp.cumprod(passed, axis=1), axis=1)
    rejected = accepted < all_len
    pick_slot = jnp.minimum(accepted, drafts - 1)[:, None]
    drafted_token = jnp.take_along_axis(all_tokens, pick_slot, axis=1)[:, 0]
    removed = jnp.where(rejected, jnp.take_along_axis(all_prob, pick_slot, axis=1)[:, 0], 0.0)
    token_prob = jnp.take_along_axis(p_draft, pick_slot, axis=1)[:, 0]
    scale_back = 1.0 - jnp.minimum(token_prob, removed)
    chosen = jnp.take_along_axis(row_of, accepted[:, None], axis=1)[:, 0]
    target_prob = jnp.exp(logits[chosen] - row_max[chosen][:, None]) / row_total[chosen][:, None]
    column_ids = my_index * columns + jnp.arange(columns, dtype=jnp.int32)
    is_drafted = column_ids[None, :] == drafted_token[:, None]
    residual = jnp.maximum(target_prob - jnp.where(is_drafted, removed[:, None], 0.0), 0.0)
    spread_rows = float(vocab_all) * residual / scale_back[:, None]
    correction = lax.all_to_all(
        spread_rows, ("vocab", "dp"), split_axis=0, concat_axis=1, tiled=True
    )
    ratio_own = lax.dynamic_slice_in_dim(accept_ratio, my_index * req_dev, req_dev, 0)
    accepted_own = lax.dynamic_slice_in_dim(accepted, my_index * req_dev, req_dev, 0)
    return (ratio_own, accepted_own, correction)


def solution(mesh):
    in_specs = (
        P(("vocab", "dp"), None),
        P(None, ("vocab", "dp")),
        P(("group", "vocab", "dp")),
        P(("vocab", "dp"), None),
        P(("vocab", "dp"), None),
        P(("group", "vocab", "dp"), None),
    )
    out_specs = (
        P(("group", "vocab", "dp"), None),
        P(("group", "vocab", "dp")),
        P(("group", "vocab", "dp"), None),
    )
    return jax.shard_map(body, mesh=mesh, in_specs=in_specs, out_specs=out_specs, check_vma=False)
```

profile of v0, /device:TPU:0, one launch (start us, length us, event | category | flops | bytes accessed | tf_op | source)
XLA Modules:
  0.0 184.2 jit_solution(12313242129015627149)
XLA Ops:
  7.2 0.7 all-gather.5.cloned.1.call-update
  7.9 23.4 %all-gather = s32[16,4,3]{2,1,0:T(4,128)S(1)} all-gather(s32[1,4,3]{2,1,0:T(4,128)} %bitcast.76), channel_id=1, replica_groups=mesh['group'=2,'vocab'=8,'dp'=2] {'vocab','dp'}, dimensions={0}, use_global_device_ids=true | all-gather | bytes 816 | tf_op jit(solution)/shard_map/all_gather | solution.py:17
  31.9 18.0 %all-gather.1 = f32[16,4,3]{2,1,0:T(4,128)S(1)} all-gather(f32[1,4,3]{2,1,0:T(4,128)} %bitcast.77), channel_id=1, replica_groups=mesh['group'=2,'vocab'=8,'dp'=2] {'vocab','dp'}, dimensions={0}, use_global_device_ids=true | all-gather | bytes 816 | tf_op jit(solution)/shard_map/all_gather | solution.py:20
  49.9 19.0 %all-gather.2 = f32[16,4,3]{2,1,0:T(4,128)S(1)} all-gather(f32[1,4,3]{2,1,0:T(4,128)} %bitcast.78), channel_id=1, replica_groups=mesh['group'=2,'vocab'=8,'dp'=2] {'vocab','dp'}, dimensions={0}, use_global_device_ids=true | all-gather | bytes 816 | tf_op jit(solution)/shard_map/all_gather | solution.py:21
  69.0 1.2 dynamic-slice
  70.9 0.9 dynamic-update-slice
  71.7 8.2 %all-reduce = s32[64]{0:T(128)S(1)} all-reduce(s32[64]{0:T(128)S(1)} %dynamic-update-slice), channel_id=1, replica_groups=mesh['group'=2,'vocab'=8,'dp'=2] {'vocab','dp'}, use_global_device_ids=true, to_apply=%add | all-reduce | flops 64 | bytes 512
  79.9 7.6 %fusion.10 = (f32[256]{0:T(256)S(1)}, f32[256,1280]{1,0:T(8,128)S(1)}) fusion(bf16[256,4096]{1,0:T(8,128)(2,1)} %all-gather.5.cloned.1.call-done, bf16[4096,1280]{1,0:T(8,128)(2,1)} %param.9), kind=kOutput, calls=%fused_computation.59 | convolution fusion | flops 2684681984 | bytes 13894656 | tf_op jit(solution)/shard_map/dot_general | solution.py:26
  87.5 31.1 %pmax.7 = f32[256]{0:T(256)S(1)} all-reduce(f32[256]{0:T(256)S(1)} %get-tuple-element.26), channel_id=1, replica_groups=mesh['group'=2,'vocab'=8,'dp'=2] {'vocab','dp'}, use_global_device_ids=true, to_apply=%region_2.3 | all-reduce | flops 256 | bytes 2048 | tf_op jit(solution)/shard_map/pmax | solution.py:37
  119.0 1.6 gather_fusion.1
  120.8 1.9 %gather_fusion = f32[192]{0:T(256)S(1)} fusion(f32[256,1280]{1,0:T(8,128)S(1)} %get-tuple-element.27, s32[192]{0:T(256)S(1)} %reshape.209), kind=kCustom, calls=%fused_computation.2 | custom fusion | bytes 3072 | tf_op jit(solution)/shard_map/gather | solution.py:36
  122.9 29.5 %all-reduce.1 = (f32[256]{0:T(256)S(1)}, f32[64,3]{0,1:T(4,128)S(1)}) all-reduce(f32[256]{0:T(256)S(1)} %exponential_reduce_fusion, f32[64,3]{0,1:T(4,128)S(1)} %and_select_fusion.2), channel_id=1, replica_groups=mesh['group'=2,'vocab'=8,'dp'=2] {'vocab','dp'}, use_global_device_ids=true, to_apply=%region_4.5 | all-reduce | flops 448 | bytes 3584 | tf_op jit(solution)/shard_map/psum | solution.py:39
  152.4 1.6 gather_fusion.2
  154.4 0.9 gather_fusion.6
  155.3 0.7 gather_fusion.3
  156.1 0.8 gather_fusion.5
  156.9 0.8 gather_fusion.4
  157.7 0.9 gather_fusion.8
  158.5 0.9 gather_fusion.9
  159.4 0.9 gather_fusion.7
  161.0 1.0 multiply_divide_fusion
  162.0 3.5 %all-to-all-start = ((f32[16,4,1280]{2,1,0:T(4,128)}), f32[16,4,1280]{2,1,0:T(4,128)S(1)}, u32[]{:S(2)}, u32[]{:S(2)}) async-start(f32[16,4,1280]{2,1,0:T(4,128)} %multiply_divide_fusion), calls=%async_computation | async-start | bytes 655360 | tf_op jit(solution)/shard_map/all_to_all | solution.py:57
  166.9 9.7 %all-to-all-done = f32[16,4,1280]{2,1,0:T(4,128)S(1)} async-done(((f32[16,4,1280]{2,1,0:T(4,128)}), f32[16,4,1280]{2,1,0:T(4,128)S(1)}, u32[]{:S(2)}, u32[]{:S(2)}) %all-to-all-start) | async-done | bytes 327712 | tf_op jit(solution)/shard_map/all_to_all | solution.py:57
  176.6 0.7 copy.55
  (48 shorter events, 3.8 us)
Async XLA Ops:
  7.2 72.8 %all-gather.5.cloned.1.call-start = ((), (), s32[]{:S(2)}) async-start(), calls=%async_computation.1 | async-start | bytes 2228224 | tf_op jit(solution)/shard_map/all_gather | solution.py:27
  162.0 14.6 %all-to-all-start = ((f32[16,4,1280]{2,1,0:T(4,128)}), f32[16,4,1280]{2,1,0:T(4,128)S(1)}, u32[]{:S(2)}, u32[]{:S(2)}) async-start(f32[16,4,1280]{2,1,0:T(4,128)} %multiply_divide_fusion), calls=%async_computation | async-start | bytes 655360 | tf_op jit(solution)/shard_map/all_to_all | solution.py:57
Sparse Core Ops, SparseCore 0:
  10.2 44.1 all-gather.4
where the time goes:
time: 184 us
  blocking collectives  129 us (70%)
  local copies, waits for them, and re-layouts  17 us (9%)
  between operations  14.9 us (8%)
  waiting for transfers between devices  10.4 us (6%)
  matrix products  7.57 us (4%)
  starting transfers between devices  3.58 us (2%)
    pmax x1, blocking collectives, body(): row_max = lax.pmax(local_max, ('vocab', 'dp'))  31.1 us
    psum x1, blocking collectives, body(): row_total, drafted = lax.psum((local_total, picked), ('vocab', 'dp'))  29.5 us
    all_gather x1, blocking collectives, body(): lax.all_gather(draft_tokens, ('vocab', 'dp'), axis=0, tiled=True)  23.4 us
    all_gather x1, blocking collectives, body(): lax.all_gather(accept_uniform, ('vocab', 'dp'), axis=0, tiled=True)  19 us
    all_gather x1, blocking collectives, body(): lax.all_gather(draft_prob, ('vocab', 'dp'), axis=0, tiled=True)  18 us
    all_to_all x1, waiting for transfers between devices, body(): lax.all_to_all(spread_rows, ('vocab', 'dp'), split_axis=0, concat_axis=1,...  9.73 us
    unnamed x1, blocking collectives  8.15 us
    dot_general x1, matrix products, body(): jnp.dot(lax.all_gather(hidden_rows, ('vocab', 'dp'), axis=0, tiled=True),...  7.57 us
  transfers between devices with their start and end apart: 2, of which 1 were waited for; matrix products, arithmetic and copies ran while one was open for 2% of the time, Pallas kernels for 0%

commit v1 on v0

v1 whole, which is shorter than its diff:
```python
import functools

import jax
import jax.numpy as jnp
from jax import lax
from jax.experimental import pallas as pl
from jax.experimental.pallas import tpu as pltpu
from jax.sharding import PartitionSpec as P

MESH = pl.DeviceIdType.MESH
CHUNKS = 4
CODE_TOP = 65535.0
CODE_STEPS = 2880.0
F32 = jnp.float32


def main_kernel(
    nv, nd,
    hid_ref, head_ref, len_ref, tok_ref, prob_ref, uni_ref,
    res_out, code_out,
    head_v, rows_v, meta_v, meta_send, acc_v, stat_v, res_v, words_v,
    head_sem, rows_recv, rows_send, meta_recv, meta_sent, stat_recv, stat_sent,
    res_recv, res_sent, code_recv, code_sent, local_sem,
):
    n = nv * nd
    total = 2 * n
    outer = nv // 2
    g = lax.axis_index("group")
    v = lax.axis_index("vocab")
    c = lax.axis_index("dp")
    h = g % 2
    base = g - h
    me = v * nd + c
    zz, yy = v // 2, v % 2
    flat = h * n + me
    half = hid_ref.shape[0] // 2
    slots = 4
    width = hid_ref.shape[1] // CHUNKS
    rows = n * half
    columns = head_ref.shape[1]

    def head_copy(k):
        at = pl.ds(k * width, width)
        return pltpu.make_async_copy(head_ref.at[at], head_v.at[at], head_sem.at[k])

    for k in range(CHUNKS):
        head_copy(k).start()

    def device_of(t):
        return (base + t // n, (t % n) // nd, t % nd)

    barrier = pltpu.get_barrier_semaphore()

    @pl.loop(1, total)
    def _(i):
        pl.semaphore_signal(barrier, inc=1, device_id=device_of((flat + i) % total), device_id_type=MESH)

    own = jnp.where(h == 0, hid_ref[0:half, :], hid_ref[half : 2 * half, :])
    for k in range(CHUNKS):
        rows_v[k * n + me] = own[:, k * width : (k + 1) * width]

    lane = lax.broadcasted_iota(jnp.int32, (half, 128), 1)
    sub = lax.broadcasted_iota(jnp.int32, (half, 128), 0)
    for part in range(2):
        block = jnp.zeros((half, 128), F32)
        for r in range(half // slots):
            req = part * (half // slots) + r
            mine = (sub // slots) == r
            block = jnp.where(mine & (lane == 3), len_ref[req].astype(F32), block)
            for s in range(slots - 1):
                at = sub == r * slots + s
                block = jnp.where(at & (lane == 0), tok_ref[req, s].astype(F32), block)
                block = jnp.where(at & (lane == 1), prob_ref[req, s], block)
                block = jnp.where(at & (lane == 2), uni_ref[req, s], block)
            at = sub == r * slots + slots - 1
            block = jnp.where(at & (lane == 0), -1.0, block)
            block = jnp.where(at & (lane == 1), 1.0, block)
        meta_send[part] = block
    meta_v[flat] = meta_send[h]

    pl.semaphore_wait(barrier, total - 1)

    def send_rows(k, src, device):
        at = k * n + src
        pltpu.make_async_remote_copy(
            rows_v.at[at], rows_v.at[at], rows_send, rows_recv.at[at], device_id=device, device_id_type=MESH
        ).start()

    def wait_rows(k, src):
        at = k * n + src
        pltpu.make_async_copy(rows_v.at[at], rows_v.at[at], rows_recv.at[at]).wait()

    for k in range(CHUNKS):
        @pl.loop(1, outer)
        def _(d):
            send_rows(k, me, (g, ((zz + d) % outer) * 2 + yy, c))

        send_rows(k, me, (g, zz * 2 + 1 - yy, c))
        send_rows(k, me, (g, v, 1 - c))

    @pl.loop(1, total)
    def _(i):
        t = (flat + i) % total
        pltpu.make_async_remote_copy(
            meta_send.at[t // n], meta_v.at[flat], meta_sent, meta_recv,
            device_id=device_of(t), device_id_type=MESH,
        ).start()

    def forward_column(k):
        @pl.loop(1, outer)
        def _(d):
            src = (((zz + d) % outer) * 2 + yy) * nd + c
            wait_rows(k, src)
            send_rows(k, src, (g, zz * 2 + 1 - yy, c))
            send_rows(k, src, (g, v, 1 - c))

    def forward_pair(k):
        @pl.loop(0, outer)
        def _(d):
            src = (((zz + d) % outer) * 2 + 1 - yy) * nd + c
            wait_rows(k, src)
            send_rows(k, src, (g, v, 1 - c))

    def multiply(k):
        @pl.loop(0, nv)
        def _(d):
            wait_rows(k, ((v + d) % nv) * nd + 1 - c)

        head_copy(k).wait()
        left = rows_v[k * n : (k + 1) * n].reshape(rows, width)

        @pl.loop(0, columns // 256)
        def _(j):
            at = pl.ds(pl.multiple_of(j * 256, 256), 256)
            product = jnp.dot(left, head_v[k * width : (k + 1) * width, at], preferred_element_type=F32)
            if k == 0:
                acc_v[:, at] = product
            else:
                acc_v[:, at] += product

    for t in range(CHUNKS + 2):
        if t < CHUNKS:
            forward_column(t)
        if 0 <= t - 1 < CHUNKS:
            forward_pair(t - 1)
        if 0 <= t - 2 < CHUNKS:
            multiply(t - 2)

    every = meta_v.at[pl.ds(0, total - 1)]
    pltpu.make_async_copy(every, every, meta_recv).wait()
    metas = [meta_v[q * n : (q + 1) * n].reshape(rows, 128) for q in range(2)]
    token, prob = metas[0][:, 0:1], metas[0][:, 1:2]

    logits = acc_v[...]
    local_max = jnp.max(logits, axis=1, keepdims=True)
    local_total = jnp.sum(jnp.exp(logits - local_max), axis=1, keepdims=True)
    column_ids = me * columns + lax.broadcasted_iota(jnp.int32, (rows, columns), 1)
    picked = jnp.sum(jnp.where(column_ids == token.astype(jnp.int32), logits, 0.0), axis=1, keepdims=True)
    wide_lane = lax.broadcasted_iota(jnp.int32, (rows, 128), 1)
    stats = jnp.where(wide_lane == 0, local_max, jnp.where(wide_lane == 1, local_total, picked))
    stat_v[me] = jnp.transpose(stats)[0:4, :]

    @pl.loop(1, n)
    def _(i):
        t = (me + i) % n
        pltpu.make_async_remote_copy(
            stat_v.at[me], stat_v.at[me], stat_sent, stat_recv,
            device_id=(g, t // nd, t % nd), device_id_type=MESH,
        ).start()

    every = stat_v.at[pl.ds(0, n - 1)]
    pltpu.make_async_copy(every, every, stat_recv).wait()
    all_stats = stat_v[...]
    all_max = all_stats[:, 0:1, :]
    top = jnp.max(all_max, axis=0)
    whole = jnp.sum(all_stats[:, 1:2, :] * jnp.exp(all_max - top[None]), axis=0)
    draft = jnp.sum(all_stats[:, 2:3, :], axis=0)
    tall = lax.broadcasted_iota(jnp.int32, (128, rows), 0)
    turned = jnp.transpose(jnp.where(tall == 0, top, jnp.where(tall == 1, whole, draft)))
    row_max, row_total, drafted = turned[:, 0:1], turned[:, 1:2], turned[:, 2:3]

    slot = lax.broadcasted_iota(jnp.int32, (rows, 1), 0) % slots
    is_draft = slot < slots - 1
    weight = jnp.where(is_draft, jnp.exp(drafted - row_max), 0.0)
    p_draft = weight / row_total
    bound = jnp.where(is_draft, jnp.minimum(1.0, 1.01 * (row_total - weight) + 1e-6), 1.0)
    origin = row_max + jnp.log(bound)
    code = jnp.clip(jnp.round((logits - origin) * CODE_STEPS) + CODE_TOP, 0.0, CODE_TOP)
    high = jnp.floor(code * (1.0 / 256.0))
    low = (code - high * 256.0).astype(jnp.bfloat16)
    high = high.astype(jnp.bfloat16)

    picks = []
    vocab_all = float(columns * n)
    requests = rows // slots
    owner = lax.broadcasted_iota(jnp.int32, (rows, requests), 0) // slots
    pick_at = lax.broadcasted_iota(jnp.int32, (rows, requests), 1)
    for q in range(2):
        uniform, length = metas[q][:, 2:3], metas[q][:, 3:4]
        live = slot.astype(F32) < length
        ratio = jnp.where(live, jnp.minimum(1.0, p_draft / prob), 0.0)
        passed = jnp.broadcast_to(jnp.where(uniform < ratio, 1.0, 0.0), (rows, 128))
        wide_slot = lax.broadcasted_iota(jnp.int32, (rows, 128), 0) % slots
        lead = passed
        for s in range(1, slots - 1):
            lead = lead * jnp.where(wide_slot >= s, pltpu.roll(passed, s, 0), 1.0)
        before = jnp.where(wide_slot == 0, 1.0, pltpu.roll(lead, 1, 0))
        chosen = before * (1.0 - lead)
        removed = jnp.where(live, prob, 0.0)
        scale = vocab_all / (1.0 - jnp.minimum(p_draft, removed))
        record = jnp.where(wide_lane == 3, slot.astype(F32), 0.0)
        record = jnp.where(wide_lane == 4, scale * bound / row_total, record)
        record = jnp.where(wide_lane == 5, scale * jnp.maximum(p_draft - removed, 0.0), record)
        record = jnp.where(wide_lane == 6, token + 1.0, record)
        record = jnp.where(chosen > 0.0, record, 0.0)
        record = jnp.where(wide_lane == wide_slot, jnp.where(wide_slot < slots - 1, ratio, record), record)
        res_v[q] = record.reshape(n, half, 128)
        picks.append(jnp.where(owner == pick_at, chosen[:, 0:1], 0.0))
    pick = jnp.concatenate(picks, axis=1).astype(jnp.bfloat16)

    to_partner = pltpu.make_async_remote_copy(
        res_v.at[1 - h, me], res_out.at[h], res_sent, res_recv,
        device_id=(base + 1 - h, v, c), device_id_type=MESH,
    )
    to_partner.start()
    to_self = pltpu.make_async_copy(res_v.at[h, me], res_out.at[h], local_sem.at[0])
    to_self.start()

    contract = (((0,), (0,)), ((), ()))
    sel_high = lax.dot_general(pick, high, contract, preferred_element_type=F32)
    sel_low = lax.dot_general(pick, low, contract, preferred_element_type=F32)
    sel = (sel_high * 256.0 + sel_low).astype(jnp.int32)
    words = sel[:, : columns // 2] | (sel[:, columns // 2 :] << 16)
    each = half // slots
    for i in range(total):
        words_v[i] = words[i * each : (i + 1) * each, :]

    @pl.loop(1, total)
    def _(i):
        t = (flat + i) % total
        pltpu.make_async_remote_copy(
            words_v.at[t], code_out.at[flat], code_sent, code_recv,
            device_id=device_of(t), device_id_type=MESH,
        ).start()

    own_words = pltpu.make_async_copy(words_v.at[flat], code_out.at[flat], local_sem.at[1])
    own_words.start()
    own_words.wait()
    to_self.wait()
    to_partner.wait()
    for ref, sem, count in (
        (rows_v, rows_send, CHUNKS * (n - 1)),
        (meta_v, meta_sent, total - 1),
        (stat_v, stat_sent, n - 1),
        (words_v, code_sent, total - 1),
        (code_out, code_recv, total - 1),
    ):
        every = ref.at[pl.ds(0, count)]
        pltpu.make_async_copy(every, every, sem).wait()


def decode_kernel(n, res_ref, code_ref, ratio_ref, accepted_ref, out_ref):
    half = res_ref.shape[1]
    slots = 4
    each = half // slots
    wide = code_ref.shape[2]
    records = []
    for h in range(2):
        for r in range(each):
            records.append(jnp.sum(res_ref[h, r * slots : (r + 1) * slots, :], axis=0, keepdims=True))
    for i, record in enumerate(records):
        accepted_ref[i] = record[0, 3].astype(jnp.int32)
    record = jnp.concatenate(records, axis=0)
    ratio_ref[...] = record[:, 0 : slots - 1]
    scale, at_token = record[:, 4:5], record[:, 5:6]
    token = record[:, 6:7].astype(jnp.int32) - 1
    ids = lax.broadcasted_iota(jnp.int32, (2 * each, wide), 1)

    @pl.loop(0, n)
    def _(i):
        word = jnp.concatenate([code_ref[i], code_ref[n + i]], axis=0)
        for part, code in enumerate((word & 65535, (word >> 16) & 65535)):
            start = pl.multiple_of((2 * i + part) * wide, 128)
            value = jnp.exp((code.astype(F32) - CODE_TOP) * (1.0 / CODE_STEPS)) * scale
            out_ref[:, pl.ds(start, wide)] = jnp.where(ids + start == token, at_token, value)


def body(hidden_rows, lm_head, draft_len, draft_tokens, draft_prob, accept_uniform):
    nv, nd = lax.axis_size("vocab"), lax.axis_size("dp")
    n = nv * nd
    half = hidden_rows.shape[0] // 2
    depth, columns = lm_head.shape
    width = depth // CHUNKS
    rows = n * half
    each = half // 4
    vmem = pl.BlockSpec(memory_space=pltpu.VMEM)
    smem = pl.BlockSpec(memory_space=pltpu.SMEM)
    dma = pltpu.SemaphoreType.DMA
    res, codes = pl.pallas_call(
        functools.partial(main_kernel, nv, nd),
        out_shape=(
            jax.ShapeDtypeStruct((2, half, 128), F32),
            jax.ShapeDtypeStruct((2 * n, each, columns // 2), jnp.int32),
        ),
        in_specs=[vmem, pl.BlockSpec(memory_space=pl.ANY), smem, smem, smem, smem],
        out_specs=(vmem, vmem),
        scratch_shapes=[
            pltpu.VMEM((depth, columns), jnp.bfloat16),
            pltpu.VMEM((CHUNKS * n, half, width), jnp.bfloat16),
            pltpu.VMEM((2 * n, half, 128), F32),
            pltpu.VMEM((2, half, 128), F32),
            pltpu.VMEM((rows, columns), F32),
            pltpu.VMEM((n, 4, rows), F32),
            pltpu.VMEM((2, n, half, 128), F32),
            pltpu.VMEM((2 * n, each, columns // 2), jnp.int32),
            dma((CHUNKS,)),
            dma((CHUNKS * n,)),
            dma, dma, dma, dma, dma, dma, dma, dma, dma,
            dma((2,)),
        ],
        compiler_params=pltpu.CompilerParams(
            collective_id=0, has_side_effects=True, vmem_limit_bytes=48 * 1024 * 1024
        ),
        name="verify",
    )(hidden_rows, lm_head, draft_len, draft_tokens, draft_prob, accept_uniform)
    return pl.pallas_call(
        functools.partial(decode_kernel, n),
        out_shape=(
            jax.ShapeDtypeStruct((2 * each, 3), F32),
            jax.ShapeDtypeStruct((2 * each,), jnp.int32),
            jax.ShapeDtypeStruct((2 * each, n * columns), F32),
        ),
        in_specs=[vmem, vmem],
        out_specs=(vmem, smem, vmem),
        name="decode",
    )(res, codes)


def solution(mesh):
    in_specs = (
        P(("vocab", "dp"), None),
        P(None, ("vocab", "dp")),
        P(("group", "vocab", "dp")),
        P(("vocab", "dp"), None),
        P(("vocab", "dp"), None),
        P(("group", "vocab", "dp"), None),
    )
    out_specs = (
        P(("group", "vocab", "dp"), None),
        P(("group", "vocab", "dp")),
        P(("group", "vocab", "dp"), None),
    )
    return jax.shard_map(body, mesh=mesh, in_specs=in_specs, out_specs=out_specs, check_vma=False)
```

time: 184 us -> 44.2 us (0.24)
  blocking collectives: 129 us -> 0 us
  Pallas kernels: 0 us -> 38.4 us
  between operations: 14.9 us -> 0.66 us
  local copies, waits for them, and re-layouts: 17 us -> 4.84 us
  waiting for transfers between devices: 10.4 us -> 0 us
  matrix products: 7.57 us -> 0 us
  starting transfers between devices: 3.58 us -> 0 us
    all_gather x3 -> x0, blocking collectives: 60.4 us -> none  [the longest x1 23.4 us: body(): lax.all_gather(draft_tokens, ('vocab', 'dp'), axis=0, tiled=True)]
    pallas_call x0 -> x2, Pallas kernels: none -> 38.4 us  [the longest x1 35.4 us: body(): pl.pallas_call(functools.partial(main_kernel, nv, nd), out_shape=(jax.Sha...]
    pmax x1 -> x0, blocking collectives: 31.1 us -> none  [body(): row_max = lax.pmax(local_max, ('vocab', 'dp'))]
    psum x1 -> x0, blocking collectives: 29.5 us -> none  [body(): row_total, drafted = lax.psum((local_total, picked), ('vocab', 'dp'))]
    gather x18 -> x0, local copies, waits for them, and re-layouts: 11.8 us -> none  [the longest x6 3.63 us: body(): p_draft = jnp.exp(drafted - row_max[draft_rows]) / row_total[draft_rows]]
    all_to_all x1 -> x0, waiting for transfers between devices: 9.73 us -> none  [body(): lax.all_to_all(spread_rows, ('vocab', 'dp'), split_axis=0, concat_axis=1,...]
    unnamed x1 -> x0, blocking collectives: 8.15 us -> none
    dot_general x1 -> x0, matrix products: 7.57 us -> none  [body(): jnp.dot(lax.all_gather(hidden_rows, ('vocab', 'dp'), axis=0, tiled=True),...]
  transfers between devices with their start and end apart: 2 -> 0, of which waited for: 1 -> 0; matrix products, arithmetic and copies ran while one was open for 2% -> 0% of each run, Pallas kernels for 0% -> 0%
where the time goes in v1:
time: 44.2 us; the launch traced here: 43.9 us
  Pallas kernels  38.4 us (87%)
  local copies, waits for them, and re-layouts  4.84 us (11%)
  between operations  0.66 us (1%)
    pallas_call x1, Pallas kernels, body(): pl.pallas_call(functools.partial(main_kernel, nv, nd), out_shape=(jax.Sha...  35.4 us
    unnamed x14, local copies, waits for them, and re-layouts  4.84 us
    pallas_call x1, Pallas kernels, body(): pl.pallas_call(functools.partial(decode_kernel, n), out_shape=(jax.ShapeD...  2.99 us

profile of v1, /device:TPU:0, one launch (start us, length us, event | category | flops | bytes accessed | tf_op | source)
XLA Modules:
  0.0 43.9 jit_solution(4982212271628393796)
XLA Ops:
  0.6 0.0 copy-start.1
  0.6 0.9 %copy-done.1 = bf16[16,4096]{1,0:T(8,128)(2,1)S(1)} copy-done((bf16[16,4096]{1,0:T(8,128)(2,1)S(1)}, bf16[16,4096]{1,0:T(8,128)(2,1)}, u32[]{:S(2)}) %copy-start.1) | copy-done | bytes 131096
  1.5 0.0 copy-start.3
  1.5 0.7 %copy-done.3 = s32[4,3]{1,0:T(4,128)S(1)} copy-done((s32[4,3]{1,0:T(4,128)S(1)}, s32[4,3]{1,0:T(4,128)}, u32[]{:S(2)}) %copy-start.3) | copy-done | bytes 72
  2.2 0.0 copy-start.4
  2.2 0.7 %copy-done.4 = f32[4,3]{1,0:T(4,128)S(1)} copy-done((f32[4,3]{1,0:T(4,128)S(1)}, f32[4,3]{1,0:T(4,128)}, u32[]{:S(2)}) %copy-start.4) | copy-done | bytes 72
  2.9 0.0 copy-start.5
  2.9 0.7 %copy-done.5 = f32[4,3]{1,0:T(4,128)S(1)} copy-done((f32[4,3]{1,0:T(4,128)S(1)}, f32[4,3]{1,0:T(4,128)}, u32[]{:S(2)}) %copy-start.5) | copy-done | bytes 72
  3.6 0.0 copy-start.6
  3.6 0.7 %copy-done.6 = s32[4]{0:T(128)S(1)} copy-done((s32[4]{0:T(128)S(1)}, s32[4]{0:T(128)}, u32[]{:S(2)}) %copy-start.6) | copy-done | bytes 40
  4.2 35.4 %verify.1 = (f32[2,8,128]{2,1,0:T(8,128)S(1)}, s32[32,2,640]{2,1,0:T(2,128)S(1)}) custom-call(bf16[16,4096]{1,0:T(8,128)(2,1)S(1)} %copy-done.1, bf16[4096,1280]{1,0:T(8,128)(2,1)} %head_ref.1, s32[4]{0:T(128)S(1)} %copy-done.6, s32[4,3]{1,0:T(4,128)S(1)} %copy-done.3, f32[4,3]{1,0:T(4,128)S(1)} %copy-done.4, f32[4,3]{1,0:T(4,128)S(1)} %copy-done.5), custom_call_target="tpu_custom_call" | custom-call | tf_op jit(solution)/shard_map/verify/pallas_call | solution.py:299
  39.6 0.0 copy-start
  39.6 0.6 %copy-done = s32[32,2,640]{2,1,0:T(2,128)} copy-done((s32[32,2,640]{2,1,0:T(2,128)}, s32[32,2,640]{2,1,0:T(2,128)S(1)}, u32[]{:S(2)}) %copy-start) | copy-done | bytes 163864
  40.3 0.0 copy-start.2
  40.3 0.6 %copy-done.2 = f32[2,8,128]{2,1,0:T(8,128)} copy-done((f32[2,8,128]{2,1,0:T(8,128)}, f32[2,8,128]{2,1,0:T(8,128)S(1)}, u32[]{:S(2)}) %copy-start.2) | copy-done | bytes 8216
  40.9 3.0 %decode.1 = (f32[4,3]{1,0:T(4,128)}, s32[4]{0:T(128)}, f32[4,20480]{1,0:T(4,128)}) custom-call(f32[2,8,128]{2,1,0:T(8,128)} %copy-done.2, s32[32,2,640]{2,1,0:T(2,128)} %copy-done), custom_call_target="tpu_custom_call" | custom-call | tf_op jit(solution)/shard_map/decode/pallas_call | solution.py:326
Async XLA Ops:
  0.6 0.9 %copy-start.1 = (bf16[16,4096]{1,0:T(8,128)(2,1)S(1)}, bf16[16,4096]{1,0:T(8,128)(2,1)}, u32[]{:S(2)}) copy-start(bf16[16,4096]{1,0:T(8,128)(2,1)} %hid_ref.1) | copy-start | bytes 393220
  1.5 0.7 %copy-start.3 = (s32[4,3]{1,0:T(4,128)S(1)}, s32[4,3]{1,0:T(4,128)}, u32[]{:S(2)}) copy-start(s32[4,3]{1,0:T(4,128)} %tok_ref.1) | copy-start | bytes 148
  2.2 0.7 %copy-start.4 = (f32[4,3]{1,0:T(4,128)S(1)}, f32[4,3]{1,0:T(4,128)}, u32[]{:S(2)}) copy-start(f32[4,3]{1,0:T(4,128)} %prob_ref.1) | copy-start | bytes 148
  2.9 0.7 %copy-start.5 = (f32[4,3]{1,0:T(4,128)S(1)}, f32[4,3]{1,0:T(4,128)}, u32[]{:S(2)}) copy-start(f32[4,3]{1,0:T(4,128)} %uni_ref.1) | copy-start | bytes 148
  3.6 0.7 %copy-start.6 = (s32[4]{0:T(128)S(1)}, s32[4]{0:T(128)}, u32[]{:S(2)}) copy-start(s32[4]{0:T(128)} %len_ref.1) | copy-start | bytes 52
  39.6 0.7 %copy-start = (s32[32,2,640]{2,1,0:T(2,128)}, s32[32,2,640]{2,1,0:T(2,128)S(1)}, u32[]{:S(2)}) copy-start(s32[32,2,640]{2,1,0:T(2,128)S(1)} %get-tuple-element.6.code_ref) | copy-start | bytes 491524
  40.3 0.6 %copy-start.2 = (f32[2,8,128]{2,1,0:T(8,128)}, f32[2,8,128]{2,1,0:T(8,128)S(1)}, u32[]{:S(2)}) copy-start(f32[2,8,128]{2,1,0:T(8,128)S(1)} %get-tuple-element.5.res_ref) | copy-start | bytes 24580

commit v2 on v1

--- a/solution.py
+++ b/solution.py
@@ -16,11 +16,11 @@
 
 def main_kernel(
     nv, nd,
-    hid_ref, head_ref, len_ref, tok_ref, prob_ref, uni_ref,
+    hid_hbm, head_ref, len_hbm, tok_hbm, prob_hbm, uni_hbm,
     res_out, code_out,
-    head_v, rows_v, meta_v, meta_send, acc_v, stat_v, res_v, words_v,
+    hid_ref, len_ref, tok_ref, prob_ref, uni_ref, head_v, rows_v, meta_v, meta_send, acc_v, stat_v, res_v, words_v,
     head_sem, rows_recv, rows_send, meta_recv, meta_sent, stat_recv, stat_sent,
-    res_recv, res_sent, code_recv, code_sent, local_sem,
+    res_recv, res_sent, code_recv, code_sent, local_sem, small_sem,
 ):
     n = nv * nd
     total = 2 * n
@@ -33,9 +33,9 @@
     me = v * nd + c
     zz, yy = v // 2, v % 2
     flat = h * n + me
-    half = hid_ref.shape[0] // 2
+    half = hid_hbm.shape[0] // 2
     slots = 4
-    width = hid_ref.shape[1] // CHUNKS
+    width = hid_hbm.shape[1] // CHUNKS
     rows = n * half
     columns = head_ref.shape[1]
 
@@ -43,6 +43,14 @@
         at = pl.ds(k * width, width)
         return pltpu.make_async_copy(head_ref.at[at], head_v.at[at], head_sem.at[k])
 
+    smalls = [
+        pltpu.make_async_copy(src, dst, small_sem.at[i])
+        for i, (src, dst) in enumerate((
+            (hid_hbm, hid_ref), (len_hbm, len_ref), (tok_hbm, tok_ref), (prob_hbm, prob_ref), (uni_hbm, uni_ref),
+        ))
+    ]
+    for copy in smalls:
+        copy.start()
     for k in range(CHUNKS):
         head_copy(k).start()
 
@@ -55,10 +63,13 @@
     def _(i):
         pl.semaphore_signal(barrier, inc=1, device_id=device_of((flat + i) % total), device_id_type=MESH)
 
+    smalls[0].wait()
     own = jnp.where(h == 0, hid_ref[0:half, :], hid_ref[half : 2 * half, :])
     for k in range(CHUNKS):
         rows_v[k * n + me] = own[:, k * width : (k + 1) * width]
 
+    for copy in smalls[1:]:
+        copy.wait()
     lane = lax.broadcasted_iota(jnp.int32, (half, 128), 1)
     sub = lax.broadcasted_iota(jnp.int32, (half, 128), 0)
     for part in range(2):
@@ -294,6 +305,7 @@
     rows = n * half
     each = half // 4
     vmem = pl.BlockSpec(memory_space=pltpu.VMEM)
+    hbm = pl.BlockSpec(memory_space=pltpu.HBM)
     smem = pl.BlockSpec(memory_space=pltpu.SMEM)
     dma = pltpu.SemaphoreType.DMA
     res, codes = pl.pallas_call(
@@ -302,9 +314,14 @@
             jax.ShapeDtypeStruct((2, half, 128), F32),
             jax.ShapeDtypeStruct((2 * n, each, columns // 2), jnp.int32),
         ),
-        in_specs=[vmem, pl.BlockSpec(memory_space=pl.ANY), smem, smem, smem, smem],
-        out_specs=(vmem, vmem),
+        in_specs=[hbm] * 6,
+        out_specs=(hbm, hbm),
         scratch_shapes=[
+            pltpu.VMEM(hidden_rows.shape, hidden_rows.dtype),
+            pltpu.SMEM(draft_len.shape, draft_len.dtype),
+            pltpu.SMEM(draft_tokens.shape, draft_tokens.dtype),
+            pltpu.SMEM(draft_prob.shape, draft_prob.dtype),
+            pltpu.SMEM(accept_uniform.shape, accept_uniform.dtype),
             pltpu.VMEM((depth, columns), jnp.bfloat16),
             pltpu.VMEM((CHUNKS * n, half, width), jnp.bfloat16),
             pltpu.VMEM((2 * n, half, 128), F32),
@@ -317,9 +334,10 @@
             dma((CHUNKS * n,)),
             dma, dma, dma, dma, dma, dma, dma, dma, dma,
             dma((2,)),
+            dma((5,)),
         ],
         compiler_params=pltpu.CompilerParams(
-            collective_id=0, has_side_effects=True, vmem_limit_bytes=48 * 1024 * 1024
+            collective_id=0, has_side_effects=True, vmem_limit_bytes=63 * 1024 * 1024
         ),
         name="verify",
     )(hidden_rows, lm_head, draft_len, draft_tokens, draft_prob, accept_uniform)
@@ -332,6 +350,7 @@
         ),
         in_specs=[vmem, vmem],
         out_specs=(vmem, smem, vmem),
+        compiler_params=pltpu.CompilerParams(vmem_limit_bytes=63 * 1024 * 1024),
         name="decode",
     )(res, codes)
 

time: 44.2 us -> 38.6 us (0.87)
  local copies, waits for them, and re-layouts: 4.84 us -> 0 us
  Pallas kernels: 38.4 us -> 37.7 us
    unnamed x14 -> x0, local copies, waits for them, and re-layouts: 4.84 us -> none
    pallas_call x1, Pallas kernels: 35.4 us -> 34.8 us  [body(): pl.pallas_call(functools.partial(main_kernel, nv, nd), out_shape=(jax.Sha...]
where the time goes in v2:
time: 38.6 us; the launch traced here: 38.4 us
  Pallas kernels  37.7 us (98%)
  between operations  0.64 us (2%)
    pallas_call x1, Pallas kernels, body(): pl.pallas_call(functools.partial(main_kernel, nv, nd), out_shape=(jax.Sha...  34.8 us
    pallas_call x1, Pallas kernels, body(): pl.pallas_call(functools.partial(decode_kernel, n), out_shape=(jax.ShapeD...  3 us

profile of v2, /device:TPU:0, one launch (start us, length us, event | category | flops | bytes accessed | tf_op | source)
XLA Modules:
  0.0 38.4 jit_solution(12515590305676959664)
XLA Ops:
  0.6 34.8 %verify.1 = (f32[2,8,128]{2,1,0:T(8,128)}, s32[32,2,640]{2,1,0:T(2,128)}) custom-call(bf16[16,4096]{1,0:T(8,128)(2,1)} %hid_hbm.1, bf16[4096,1280]{1,0:T(8,128)(2,1)} %head_ref.1, s32[4]{0:T(128)} %len_hbm.1, s32[4,3]{1,0:T(4,128)} %tok_hbm.1, f32[4,3]{1,0:T(4,128)} %prob_hbm.1, f32[4,3]{1,0:T(4,128)} %uni_hbm.1), custom_call_target="tpu_custom_call" | custom-call | tf_op jit(solution)/shard_map/verify/pallas_call | solution.py:311
  35.4 3.0 %decode.1 = (f32[4,3]{1,0:T(4,128)}, s32[4]{0:T(128)}, f32[4,20480]{1,0:T(4,128)}) custom-call(f32[2,8,128]{2,1,0:T(8,128)} %get-tuple-element.5.res_ref, s32[32,2,640]{2,1,0:T(2,128)} %get-tuple-element.6.code_ref), custom_call_target="tpu_custom_call" | custom-call | tf_op jit(solution)/shard_map/decode/pallas_call | solution.py:344

commit v3 on v2

--- a/solution.py
+++ b/solution.py
@@ -9,6 +9,7 @@
 
 MESH = pl.DeviceIdType.MESH
 CHUNKS = 4
+FIELDS = 128
 CODE_TOP = 65535.0
 CODE_STEPS = 2880.0
 F32 = jnp.float32
@@ -18,8 +19,8 @@
     nv, nd,
     hid_hbm, head_ref, len_hbm, tok_hbm, prob_hbm, uni_hbm,
     res_out, code_out,
-    hid_ref, len_ref, tok_ref, prob_ref, uni_ref, head_v, rows_v, meta_v, meta_send, acc_v, stat_v, res_v, words_v,
-    head_sem, rows_recv, rows_send, meta_recv, meta_sent, stat_recv, stat_sent,
+    hid_ref, len_ref, tok_ref, prob_ref, uni_ref, head_v, rows_a, rows_b, meta_in, meta_send, acc_v, stat_v, res_v, words_v,
+    head_sem, rows_recv, rows_send, pair_recv, core_recv, meta_recv, meta_sent, stat_recv, stat_sent,
     res_recv, res_sent, code_recv, code_sent, local_sem, small_sem,
 ):
     n = nv * nd
@@ -33,6 +34,7 @@
     me = v * nd + c
     zz, yy = v // 2, v % 2
     flat = h * n + me
+    spot = (yy * nd + c) * outer + zz
     half = hid_hbm.shape[0] // 2
     slots = 4
     width = hid_hbm.shape[1] // CHUNKS
@@ -54,19 +56,38 @@
     for k in range(CHUNKS):
         head_copy(k).start()
 
-    def device_of(t):
-        return (base + t // n, (t % n) // nd, t % nd)
+    def plane_peers(visit, planes):
+        def around(tz, first):
+            for py in range(2):
+                ty = yy if py == 0 else 1 - yy
+                for pc in range(2):
+                    tc = c if pc == 0 else 1 - c
+                    for ph in range(planes):
+                        th = h if ph == 0 else 1 - h
+                        if not (first and py == pc == ph == 0):
+                            visit((base + th, tz * 2 + ty, tc), th, (ty * nd + tc) * outer + tz)
+
+        around(zz, True)
+
+        @pl.loop(1, outer)
+        def _(d):
+            tz = zz + d
+            around(jnp.where(tz >= outer, tz - outer, tz), False)
 
     barrier = pltpu.get_barrier_semaphore()
 
-    @pl.loop(1, total)
-    def _(i):
-        pl.semaphore_signal(barrier, inc=1, device_id=device_of((flat + i) % total), device_id_type=MESH)
+    def greet(device, plane, place):
+        pl.semaphore_signal(barrier, inc=1, device_id=device, device_id_type=MESH)
+
+    plane_peers(greet, 2)
 
     smalls[0].wait()
     own = jnp.where(h == 0, hid_ref[0:half, :], hid_ref[half : 2 * half, :])
+    def rows_of(k):
+        return rows_b if k == CHUNKS - 1 else rows_a.at[k]
+
     for k in range(CHUNKS):
-        rows_v[k * n + me] = own[:, k * width : (k + 1) * width]
+        rows_of(k)[spot, :, 0:width] = own[:, k * width : (k + 1) * width]
 
     for copy in smalls[1:]:
         copy.wait()
@@ -87,58 +108,61 @@
             block = jnp.where(at & (lane == 0), -1.0, block)
             block = jnp.where(at & (lane == 1), 1.0, block)
         meta_send[part] = block
-    meta_v[flat] = meta_send[h]
-
     pl.semaphore_wait(barrier, total - 1)
 
-    def send_rows(k, src, device):
-        at = k * n + src
-        pltpu.make_async_remote_copy(
-            rows_v.at[at], rows_v.at[at], rows_send, rows_recv.at[at], device_id=device, device_id_type=MESH
-        ).start()
-
-    def wait_rows(k, src):
-        at = k * n + src
-        pltpu.make_async_copy(rows_v.at[at], rows_v.at[at], rows_recv.at[at]).wait()
-
-    for k in range(CHUNKS):
+    meta_swap = pltpu.make_async_remote_copy(
+        meta_send.at[1 - h], meta_in, meta_sent, meta_recv,
+        device_id=(base + 1 - h, v, c), device_id_type=MESH,
+    )
+    meta_swap.start()
+
+    def send_column(k):
         @pl.loop(1, outer)
         def _(d):
-            send_rows(k, me, (g, ((zz + d) % outer) * 2 + yy, c))
-
-        send_rows(k, me, (g, zz * 2 + 1 - yy, c))
-        send_rows(k, me, (g, v, 1 - c))
-
-    @pl.loop(1, total)
-    def _(i):
-        t = (flat + i) % total
+            tz = zz + d
+            tz = jnp.where(tz >= outer, tz - outer, tz)
+            pltpu.make_async_remote_copy(
+                rows_of(k).at[spot], rows_of(k).at[spot], rows_send.at[k], rows_recv.at[k],
+                device_id=(g, tz * 2 + yy, c), device_id_type=MESH,
+            ).start()
+
+    def send_four(k, y, recv, device):
+        at = pl.ds((y * nd + c) * outer, outer)
         pltpu.make_async_remote_copy(
-            meta_send.at[t // n], meta_v.at[flat], meta_sent, meta_recv,
-            device_id=device_of(t), device_id_type=MESH,
+            rows_of(k).at[at], rows_of(k).at[at], rows_send.at[k], recv, device_id=device, device_id_type=MESH
         ).start()
 
+    def wait_blocks(k, count, sem):
+        some = rows_of(k).at[pl.ds(0, count)]
+        pltpu.make_async_copy(some, some, sem).wait()
+
+    for k in range(CHUNKS - 1):
+        send_column(k)
+    meta_swap.wait()
+    own_part, other_part = meta_send[h], meta_in[...]
+    parts = [jnp.where(h == 0, own_part, other_part), jnp.where(h == 0, other_part, own_part)]
+    fields = jnp.where(lane < 4, parts[0], jnp.where(lane < 6, pltpu.roll(parts[1], 2, 1), 0.0))
+    piece = fields.astype(jnp.bfloat16).astype(F32)
+    left_over = fields - piece
+    second = left_over.astype(jnp.bfloat16).astype(F32)
+    pieces = piece + pltpu.roll(second, 8, 1) + pltpu.roll(left_over - second, 16, 1)
+    rows_b[spot, :, width : width + FIELDS] = pieces.astype(jnp.bfloat16)
+    send_column(CHUNKS - 1)
+
     def forward_column(k):
-        @pl.loop(1, outer)
-        def _(d):
-            src = (((zz + d) % outer) * 2 + yy) * nd + c
-            wait_rows(k, src)
-            send_rows(k, src, (g, zz * 2 + 1 - yy, c))
-            send_rows(k, src, (g, v, 1 - c))
+        wait_blocks(k, outer - 1, rows_recv.at[k])
+        send_four(k, yy, pair_recv.at[k], (g, zz * 2 + 1 - yy, c))
+        send_four(k, yy, core_recv.at[2 * k], (g, v, 1 - c))
 
     def forward_pair(k):
-        @pl.loop(0, outer)
-        def _(d):
-            src = (((zz + d) % outer) * 2 + 1 - yy) * nd + c
-            wait_rows(k, src)
-            send_rows(k, src, (g, v, 1 - c))
+        wait_blocks(k, outer, pair_recv.at[k])
+        send_four(k, 1 - yy, core_recv.at[2 * k + 1], (g, v, 1 - c))
 
     def multiply(k):
-        @pl.loop(0, nv)
-        def _(d):
-            wait_rows(k, ((v + d) % nv) * nd + 1 - c)
-
+        wait_blocks(k, outer, core_recv.at[2 * k])
+        wait_blocks(k, outer, core_recv.at[2 * k + 1])
         head_copy(k).wait()
-        left = rows_v[k * n : (k + 1) * n].reshape(rows, width)
+        left = rows_of(k)[:, :, 0:width].reshape(rows, width)
 
         @pl.loop(0, columns // 256)
         def _(j):
@@ -157,10 +181,9 @@
         if 0 <= t - 2 < CHUNKS:
             multiply(t - 2)
 
-    every = meta_v.at[pl.ds(0, total - 1)]
-    pltpu.make_async_copy(every, every, meta_recv).wait()
-    metas = [meta_v[q * n : (q + 1) * n].reshape(rows, 128) for q in range(2)]
-    token, prob = metas[0][:, 0:1], metas[0][:, 1:2]
+    numbers = rows_b[:, :, width : width + FIELDS].reshape(rows, FIELDS).astype(F32)
+    numbers = numbers + pltpu.roll(numbers, FIELDS - 8, 1) + pltpu.roll(numbers, FIELDS - 16, 1)
+    token, prob = numbers[:, 0:1], numbers[:, 1:2]
 
     logits = acc_v[...]
     local_max = jnp.max(logits, axis=1, keepdims=True)
@@ -171,13 +194,12 @@
     stats = jnp.where(wide_lane == 0, local_max, jnp.where(wide_lane == 1, local_total, picked))
     stat_v[me] = jnp.transpose(stats)[0:4, :]
 
-    @pl.loop(1, n)
-    def _(i):
-        t = (me + i) % n
+    def send_stats(device, plane, place):
         pltpu.make_async_remote_copy(
-            stat_v.at[me], stat_v.at[me], stat_sent, stat_recv,
-            device_id=(g, t // nd, t % nd), device_id_type=MESH,
+            stat_v.at[me], stat_v.at[me], stat_sent, stat_recv, device_id=device, device_id_type=MESH
         ).start()
+
+    plane_peers(send_stats, 1)
 
     every = stat_v.at[pl.ds(0, n - 1)]
     pltpu.make_async_copy(every, every, stat_recv).wait()
@@ -207,7 +229,7 @@
     owner = lax.broadcasted_iota(jnp.int32, (rows, requests), 0) // slots
     pick_at = lax.broadcasted_iota(jnp.int32, (rows, requests), 1)
     for q in range(2):
-        uniform, length = metas[q][:, 2:3], metas[q][:, 3:4]
+        uniform, length = numbers[:, 2 + 2 * q : 3 + 2 * q], numbers[:, 3 + 2 * q : 4 + 2 * q]
         live = slot.astype(F32) < length
         ratio = jnp.where(live, jnp.minimum(1.0, p_draft / prob), 0.0)
         passed = jnp.broadcast_to(jnp.where(uniform < ratio, 1.0, 0.0), (rows, 128))
@@ -230,11 +252,11 @@
     pick = jnp.concatenate(picks, axis=1).astype(jnp.bfloat16)
 
     to_partner = pltpu.make_async_remote_copy(
-        res_v.at[1 - h, me], res_out.at[h], res_sent, res_recv,
+        res_v.at[1 - h, spot], res_out.at[h], res_sent, res_recv,
         device_id=(base + 1 - h, v, c), device_id_type=MESH,
     )
     to_partner.start()
-    to_self = pltpu.make_async_copy(res_v.at[h, me], res_out.at[h], local_sem.at[0])
+    to_self = pltpu.make_async_copy(res_v.at[h, spot], res_out.at[h], local_sem.at[0])
     to_self.start()
 
     contract = (((0,), (0,)), ((), ()))
@@ -246,22 +268,22 @@
     for i in range(total):
         words_v[i] = words[i * each : (i + 1) * each, :]
 
-    @pl.loop(1, total)
-    def _(i):
-        t = (flat + i) % total
+    def send_words(device, plane, place):
         pltpu.make_async_remote_copy(
-            words_v.at[t], code_out.at[flat], code_sent, code_recv,
-            device_id=device_of(t), device_id_type=MESH,
+            words_v.at[plane * n + place], code_out.at[flat], code_sent, code_recv,
+            device_id=device, device_id_type=MESH,
         ).start()
 
-    own_words = pltpu.make_async_copy(words_v.at[flat], code_out.at[flat], local_sem.at[1])
+    plane_peers(send_words, 2)
+
+    own_words = pltpu.make_async_copy(words_v.at[h * n + spot], code_out.at[flat], local_sem.at[1])
     own_words.start()
     own_words.wait()
     to_self.wait()
     to_partner.wait()
+    for k in range(CHUNKS):
+        wait_blocks(k, n - 1, rows_send.at[k])
     for ref, sem, count in (
-        (rows_v, rows_send, CHUNKS * (n - 1)),
-        (meta_v, meta_sent, total - 1),
         (stat_v, stat_sent, n - 1),
         (words_v, code_sent, total - 1),
         (code_out, code_recv, total - 1),
@@ -323,16 +345,20 @@
             pltpu.SMEM(draft_prob.shape, draft_prob.dtype),
             pltpu.SMEM(accept_uniform.shape, accept_uniform.dtype),
             pltpu.VMEM((depth, columns), jnp.bfloat16),
-            pltpu.VMEM((CHUNKS * n, half, width), jnp.bfloat16),
-            pltpu.VMEM((2 * n, half, 128), F32),
+            pltpu.VMEM((CHUNKS - 1, n, half, width), jnp.bfloat16),
+            pltpu.VMEM((n, half, width + FIELDS), jnp.bfloat16),
+            pltpu.VMEM((half, 128), F32),
             pltpu.VMEM((2, half, 128), F32),
             pltpu.VMEM((rows, columns), F32),
             pltpu.VMEM((n, 4, rows), F32),
             pltpu.VMEM((2, n, half, 128), F32),
             pltpu.VMEM((2 * n, each, columns // 2), jnp.int32),
             dma((CHUNKS,)),
-            dma((CHUNKS * n,)),
-            dma, dma, dma, dma, dma, dma, dma, dma, dma,
+            dma((CHUNKS,)),
+            dma((CHUNKS,)),
+            dma((CHUNKS,)),
+            dma((2 * CHUNKS,)),
+            dma, dma, dma, dma, dma, dma, dma, dma,
             dma((2,)),
             dma((5,)),
         ],

time: 38.6 us -> 38.5 us (level)
  no operation moved by 1% of the time
where the time goes in v3:
time: 38.5 us; the launch traced here: 38.3 us
  Pallas kernels  37.7 us (98%)
  between operations  0.64 us (2%)
    pallas_call x1, Pallas kernels, body(): pl.pallas_call(functools.partial(main_kernel, nv, nd), out_shape=(jax.Sha...  34.7 us
    pallas_call x1, Pallas kernels, body(): pl.pallas_call(functools.partial(decode_kernel, n), out_shape=(jax.ShapeD...  3 us

profile of v3, /device:TPU:0, one launch (start us, length us, event | category | flops | bytes accessed | tf_op | source)
XLA Modules:
  0.0 38.3 jit_solution(9517724290135336267)
XLA Ops:
  0.6 34.7 %verify.1 = (f32[2,8,128]{2,1,0:T(8,128)}, s32[32,2,640]{2,1,0:T(2,128)}) custom-call(bf16[16,4096]{1,0:T(8,128)(2,1)} %hid_hbm.1, bf16[4096,1280]{1,0:T(8,128)(2,1)} %head_ref.1, s32[4]{0:T(128)} %len_hbm.1, s32[4,3]{1,0:T(4,128)} %tok_hbm.1, f32[4,3]{1,0:T(4,128)} %prob_hbm.1, f32[4,3]{1,0:T(4,128)} %uni_hbm.1), custom_call_target="tpu_custom_call" | custom-call | tf_op jit(solution)/shard_map/verify/pallas_call | solution.py:333
  35.3 3.0 %decode.1 = (f32[4,3]{1,0:T(4,128)}, s32[4]{0:T(128)}, f32[4,20480]{1,0:T(4,128)}) custom-call(f32[2,8,128]{2,1,0:T(8,128)} %get-tuple-element.5.res_ref, s32[32,2,640]{2,1,0:T(2,128)} %get-tuple-element.6.code_ref), custom_call_target="tpu_custom_call" | custom-call | tf_op jit(solution)/shard_map/decode/pallas_call | solution.py:370

commit v4 on v3

--- a/solution.py
+++ b/solution.py
@@ -309,13 +309,12 @@
     token = record[:, 6:7].astype(jnp.int32) - 1
     ids = lax.broadcasted_iota(jnp.int32, (2 * each, wide), 1)
 
-    @pl.loop(0, n)
-    def _(i):
+    for i in range(n):
         word = jnp.concatenate([code_ref[i], code_ref[n + i]], axis=0)
         for part, code in enumerate((word & 65535, (word >> 16) & 65535)):
-            start = pl.multiple_of((2 * i + part) * wide, 128)
+            start = (2 * i + part) * wide
             value = jnp.exp((code.astype(F32) - CODE_TOP) * (1.0 / CODE_STEPS)) * scale
-            out_ref[:, pl.ds(start, wide)] = jnp.where(ids + start == token, at_token, value)
+            out_ref[:, start : start + wide] = jnp.where(ids + start == token, at_token, value)
 
 
 def body(hidden_rows, lm_head, draft_len, draft_tokens, draft_prob, accept_uniform):

time: 38.5 us -> 37.5 us (0.974)
  Pallas kernels: 37.7 us -> 36.6 us
    pallas_call x1, Pallas kernels: 3 us -> 1.97 us  [body(): pl.pallas_call(functools.partial(decode_kernel, n), out_shape=(jax.ShapeD...]
where the time goes in v4:
time: 37.5 us; the launch traced here: 37.3 us
  Pallas kernels  36.6 us (98%)
  between operations  0.64 us (2%)
    pallas_call x1, Pallas kernels, body(): pl.pallas_call(functools.partial(main_kernel, nv, nd), out_shape=(jax.Sha...  34.7 us
    pallas_call x1, Pallas kernels, body(): pl.pallas_call(functools.partial(decode_kernel, n), out_shape=(jax.ShapeD...  1.97 us

profile of v4, /device:TPU:0, one launch (start us, length us, event | category | flops | bytes accessed | tf_op | source)
XLA Modules:
  0.0 37.3 jit_solution(10697153927049366184)
XLA Ops:
  0.6 34.7 %verify.1 = (f32[2,8,128]{2,1,0:T(8,128)}, s32[32,2,640]{2,1,0:T(2,128)}) custom-call(bf16[16,4096]{1,0:T(8,128)(2,1)} %hid_hbm.1, bf16[4096,1280]{1,0:T(8,128)(2,1)} %head_ref.1, s32[4]{0:T(128)} %len_hbm.1, s32[4,3]{1,0:T(4,128)} %tok_hbm.1, f32[4,3]{1,0:T(4,128)} %prob_hbm.1, f32[4,3]{1,0:T(4,128)} %uni_hbm.1), custom_call_target="tpu_custom_call" | custom-call | tf_op jit(solution)/shard_map/verify/pallas_call | solution.py:332
  35.3 2.0 %decode.1 = (f32[4,3]{1,0:T(4,128)}, s32[4]{0:T(128)}, f32[4,20480]{1,0:T(4,128)}) custom-call(f32[2,8,128]{2,1,0:T(8,128)} %get-tuple-element.5.res_ref, s32[32,2,640]{2,1,0:T(2,128)} %get-tuple-element.6.code_ref), custom_call_target="tpu_custom_call" | custom-call | tf_op jit(solution)/shard_map/decode/pallas_call | solution.py:369
